TPU v7x, 32 devices: a whole 2x2x4 slice. The times are simulated.
32 devices in a mesh: elem: 8 (over z, y), orb: 4 (over x, core).
Axes of the slice: x: 2, y: 2, z: 4, core: 2. Of those that a mesh axis runs over, the one named last changes fastest.
Arguments:
- hamiltonian: bfloat16 [256, 7, 128, 128], P('elem'), may hold values from -1 to 1, as said below
- start: bfloat16 [256, 128, 1024], P('elem', None, 'orb'), may hold values from -6 to 6
- ritz: bfloat16 [1024, 1024], P(None, 'orb'), may hold values from -0.1875 to 0.1875
Outputs:
- margin: float32 [1024, 1024], P('orb', 'elem')
- rotated: float32 [256, 128, 1024], P('elem', None, 'orb')
Inputs may be any that keep to these rules, and one draw needn't show every extreme that they name: hamiltonian[e, 1 + 2 k] is the transpose of hamiltonian[n(e, 1 + 2 k), 2 + 2 k], and each diagonal block hamiltonian[e, 0] is symmetric, so the operator is symmetric.
All inputs are finite; a program needn't handle non-finite values.
Results may differ from a plain program's by a relative error of at most 0.0095.
Values may be sent and summed in bfloat16 or wider, within the bound.
A program may use at most 128 MiB of HBM per device.

v0:
```python
import jax
import jax.numpy as jnp
from jax import lax
from jax.sharding import PartitionSpec as P

NB = 128
GY = 4
GZ = 4
DEG = 6


center_shift = 0.1
half_width = 1.25


def extended(cells, sides, width):
    for axis, dim in sides:
        count = lax.axis_size(axis)
        head = lax.slice_in_dim(cells, 0, width, axis=dim)
        tail = lax.slice_in_dim(cells, cells.shape[dim] - width, cells.shape[dim], axis=dim)
        cells = jnp.concatenate(
            [
                lax.ppermute(tail, axis, [(i, (i + 1) % count) for i in range(count)]),
                cells,
                lax.ppermute(head, axis, [((i + 1) % count, i) for i in range(count)]),
            ],
            axis=dim,
        )
    return cells


def apply_ham(hamiltonian, rounded):
    elem_count = hamiltonian.shape[0]
    orb_cols = rounded.shape[2]
    layers = elem_count // (GY * GZ)
    element_grid = rounded.reshape(layers, GY, GZ, NB, orb_cols)
    padded = extended(element_grid, (("elem", 0),), 1)
    neighbours = [
        element_grid,
        padded[:-2],
        padded[2:],
        jnp.roll(element_grid, 1, axis=1),
        jnp.roll(element_grid, -1, axis=1),
        jnp.roll(element_grid, 1, axis=2),
        jnp.roll(element_grid, -1, axis=2),
    ]
    accumulated = jnp.zeros((elem_count, NB, orb_cols), jnp.float32)
    for direction in range(7):
        moved = neighbours[direction].reshape(elem_count, NB, orb_cols)
        accumulated = accumulated + jnp.einsum(
            "eij,ejo->eio", hamiltonian[:, direction], moved, preferred_element_type=jnp.float32
        )
    return accumulated


def on_device(hamiltonian, start, ritz):
    elem_count = hamiltonian.shape[0]
    orb_cols = start.shape[2]
    local_rows = elem_count * NB
    rows_total = float(local_rows * lax.axis_size("elem"))
    previous = start.astype(jnp.float32)
    current = (apply_ham(hamiltonian, start) - center_shift * previous) / half_width
    for degree in range(DEG - 1):
        rounded = current.astype(jnp.bfloat16)
        image = apply_ham(hamiltonian, rounded)
        following = 2.0 / half_width * (image - center_shift * current) - previous
        previous = current
        current = following
    filtered = current.astype(jnp.bfloat16).reshape(local_rows, orb_cols)
    panel_cols = lax.all_gather(filtered, "orb", axis=1, tiled=True)
    block_part = jnp.einsum("ri,rj->ij", filtered, panel_cols, preferred_element_type=jnp.float32)
    margin_rows = block_part
    rotated_part = jnp.dot(panel_cols, ritz, preferred_element_type=jnp.float32)
    margin_rows, rotated_local = (margin_rows, rotated_part)
    margin_block = (
        lax.psum_scatter(
            margin_rows.astype(jnp.bfloat16), "elem", scatter_dimension=1, tiled=True
        ).astype(jnp.float32)
        / rows_total
    )
    return (margin_block, rotated_local.reshape(elem_count, NB, orb_cols))


def solution(mesh):
    in_specs = (P("elem", None, None, None), P("elem", None, "orb"), P(None, "orb"))
    out_specs = (P("orb", "elem"), P("elem", None, "orb"))
    return jax.shard_map(
        on_device, mesh=mesh, in_specs=in_specs, out_specs=out_specs, check_vma=False
    )
```

profile of v0, /device:TPU:0, one launch (start us, length us, event | category | flops | bytes accessed | tf_op | source)
XLA Modules:
  0.0 566.0 jit_solution(4609076412858724543)
XLA Ops:
  9.1 3.0 collective-permute-start
  12.2 3.1 collective-permute-start.1
  30.8 26.2 %collective-permute-done = bf16[1,4,4,128,256]{4,3,2,1,0:T(8,128)(2,1)S(1)} collective-permute-done((bf16[1,4,4,128,256]{4,3,2,1,0:T(8,128)(2,1)S(1)}, bf16[1,4,4,128,256]{4,3,2,1,0:T(8,128)(2,1)S(1)}, u32[]{:S(2)}, u32[]{:S(2)}) %collective-permute-start) | collective-permute-done | bytes 1048608 | tf_op jit(solution)/shard_map/ppermute | solution.py:23
  63.7 10.8 %multiply_convert_fusion = (bf16[32,128,256]{2,1,0:T(8,128)(2,1)S(1)}, f32[32,128,256]{2,1,0:T(8,128)}) fusion(bf16[32,128,256]{2,1,0:T(8,128)(2,1)S(1)} %copy-done.1, f32[32,256,128]{1,2,0:T(8,128)} %fusion.11, f32[32,256,128]{1,2,0:T(8,128)} %fusion.23, f32[32,256,128]{1,2,0:T(8,128)} %fusion.35, f32[32,256,128]{1,2,0:T(8,128)} %fusion.47, ...), kind=kOutput, calls=%fused_computation.24 | convolution fusion | flops 279969792 | bytes 36700160 | tf_op jit(solution)/shard_map/eij,ejo->eio/dot_general | solution.py:50
  78.5 4.6 collective-permute-start.3
  86.2 2.8 fusion.49
  94.8 27.7 %collective-permute-done.2 = bf16[1,4,4,128,256]{4,3,2,1,0:T(8,128)(2,1)S(1)} collective-permute-done((bf16[1,4,4,128,256]{4,3,2,1,0:T(8,128)(2,1)S(1)}, bf16[1,4,4,128,256]{4,3,2,1,0:T(8,128)(2,1)S(1)}, u32[]{:S(2)}, u32[]{:S(2)}) %collective-permute-start.2) | collective-permute-done | bytes 1048608 | tf_op jit(solution)/shard_map/ppermute | solution.py:23
  122.5 4.1 collective-permute-done.3
  131.1 14.0 %fusion.161 = (bf16[32,128,256]{2,1,0:T(8,128)(2,1)}, f32[32,128,256]{2,1,0:T(8,128)}) fusion(bf16[32,128,256]{2,1,0:T(8,128)(2,1)S(1)} %copy-done.1, f32[32,128,256]{2,1,0:T(8,128)} %get-tuple-element.75, f32[32,256,128]{1,2,0:T(8,128)} %fusion.13, f32[32,256,128]{1,2,0:T(8,128)} %fusion.25, f32[32,256,128]{1,2,0:T(8,128)} %fusion.37, ...), kind=kOutput, calls=%fused_computation.213 | convolution fusion | flops 281018368 | bytes 40894464 | tf_op jit(solution)/shard_map/eij,ejo->eio/dot_general | solution.py:50
  150.8 5.0 collective-permute-start.5
  164.6 2.8 fusion.27
  167.4 28.3 %collective-permute-done.4 = bf16[1,4,4,128,256]{4,3,2,1,0:T(8,128)(2,1)S(1)} collective-permute-done((bf16[1,4,4,128,256]{4,3,2,1,0:T(8,128)(2,1)S(1)}, bf16[1,4,4,128,256]{4,3,2,1,0:T(8,128)(2,1)S(1)}, u32[]{:S(2)}, u32[]{:S(2)}) %collective-permute-start.4) | collective-permute-done | bytes 1048608 | tf_op jit(solution)/shard_map/ppermute | solution.py:23
  195.7 3.6 collective-permute-done.5
  203.8 14.5 %fusion.162 = (bf16[32,128,256]{2,1,0:T(8,128)(2,1)S(1)}, f32[32,128,256]{2,1,0:T(8,128)}) fusion(f32[32,128,256]{2,1,0:T(8,128)} %get-tuple-element.75, f32[32,128,256]{2,1,0:T(8,128)} %get-tuple-element.77, f32[32,256,128]{1,2,0:T(8,128)} %fusion.15, f32[32,256,128]{1,2,0:T(8,128)} %fusion.27, f32[32,256,128]{1,2,0:T(8,128)} %fusion.39, ...), kind=kOutput, calls=%fused_computation.214 | convolution fusion | flops 281018368 | bytes 42991616 | tf_op jit(solution)/shard_map/eij,ejo->eio/dot_general | solution.py:50
  222.2 5.2 collective-permute-start.7
  239.0 27.7 %collective-permute-done.6 = bf16[1,4,4,128,256]{4,3,2,1,0:T(8,128)(2,1)S(1)} collective-permute-done((bf16[1,4,4,128,256]{4,3,2,1,0:T(8,128)(2,1)S(1)}, bf16[1,4,4,128,256]{4,3,2,1,0:T(8,128)(2,1)S(1)}, u32[]{:S(2)}, u32[]{:S(2)}) %collective-permute-start.6) | collective-permute-done | bytes 1048608 | tf_op jit(solution)/shard_map/ppermute | solution.py:23
  266.7 4.2 collective-permute-done.7
  272.7 2.8 fusion.71
  275.4 14.5 %fusion.163 = (bf16[32,128,256]{2,1,0:T(8,128)(2,1)S(1)}, f32[32,128,256]{2,1,0:T(8,128)}) fusion(f32[32,128,256]{2,1,0:T(8,128)} %get-tuple-element.77, f32[32,128,256]{2,1,0:T(8,128)} %get-tuple-element.79, f32[32,256,128]{1,2,0:T(8,128)} %fusion.17, f32[32,256,128]{1,2,0:T(8,128)} %fusion.29, f32[32,256,128]{1,2,0:T(8,128)} %fusion.41, ...), kind=kOutput, calls=%fused_computation.215 | convolution fusion | flops 279969792 | bytes 42991616 | tf_op jit(solution)/shard_map/eij,ejo->eio/dot_general | solution.py:50
  293.9 4.9 collective-permute-start.9
  307.5 2.8 fusion.31
  310.3 28.2 %collective-permute-done.8 = bf16[1,4,4,128,256]{4,3,2,1,0:T(8,128)(2,1)S(1)} collective-permute-done((bf16[1,4,4,128,256]{4,3,2,1,0:T(8,128)(2,1)S(1)}, bf16[1,4,4,128,256]{4,3,2,1,0:T(8,128)(2,1)S(1)}, u32[]{:S(2)}, u32[]{:S(2)}) %collective-permute-start.8) | collective-permute-done | bytes 1048608 | tf_op jit(solution)/shard_map/ppermute | solution.py:23
  345.6 14.5 %fusion.164 = (bf16[32,128,256]{2,1,0:T(8,128)(2,1)S(1)}, f32[32,128,256]{2,1,0:T(8,128)}) fusion(f32[32,128,256]{2,1,0:T(8,128)} %get-tuple-element.79, f32[32,128,256]{2,1,0:T(8,128)} %get-tuple-element.81, f32[32,256,128]{1,2,0:T(8,128)} %fusion.19, f32[32,256,128]{1,2,0:T(8,128)} %fusion.31, f32[32,256,128]{1,2,0:T(8,128)} %fusion.43, ...), kind=kOutput, calls=%fused_computation.216 | convolution fusion | flops 279969792 | bytes 42991616 | tf_op jit(solution)/shard_map/eij,ejo->eio/dot_general | solution.py:50
  364.0 4.9 collective-permute-start.11
  377.8 2.8 fusion.33
  380.5 27.4 %collective-permute-done.10 = bf16[1,4,4,128,256]{4,3,2,1,0:T(8,128)(2,1)S(1)} collective-permute-done((bf16[1,4,4,128,256]{4,3,2,1,0:T(8,128)(2,1)S(1)}, bf16[1,4,4,128,256]{4,3,2,1,0:T(8,128)(2,1)S(1)}, u32[]{:S(2)}, u32[]{:S(2)}) %collective-permute-start.10) | collective-permute-done | bytes 1048608 | tf_op jit(solution)/shard_map/ppermute | solution.py:23
  408.0 4.2 collective-permute-done.11
  416.8 13.0 %fusion.3 = bf16[32,128,256]{2,1,0:T(8,128)(2,1)} fusion(f32[32,128,256]{2,1,0:T(8,128)} %get-tuple-element.81, f32[32,256,128]{1,2,0:T(8,128)} %fusion.21, f32[32,256,128]{1,2,0:T(8,128)} %fusion.33, f32[32,128,256]{2,1,0:T(8,128)} %get-tuple-element.83, f32[32,256,128]{1,2,0:T(8,128)} %fusion.45, f32[32,256,128]{1,2,0:T(8,128)} %fusion.57, ...), kind=kOutput, calls=%fused_computation.6 | convolution fusion | flops 279969792 | bytes 38797312 | tf_op jit(solution)/shard_map/eij,ejo->eio/dot_general | solution.py:50
  429.9 58.6 %all-gather.2.cloned.1.call-done = bf16[4096,1024]{1,0:T(8,128)(2,1)} async-done(((bf16[4096,256]{1,0:T(8,128)(2,1)}), bf16[4096,1024]{1,0:T(8,128)(2,1)}) %all-gather.2.cloned.1.call-update) | async-done | bytes 8388624 | tf_op jit(solution)/shard_map/all_gather | solution.py:70
  488.4 5.7 %convolution_convert_fusion = bf16[256,1024]{1,0:T(8,128)(2,1)S(1)} fusion(bf16[4096,256]{1,0:T(8,128)(2,1)S(1)} %bitcast.308, bf16[4096,1024]{1,0:T(8,128)(2,1)} %all-gather.2.cloned.1.call-done), kind=kOutput, calls=%fused_computation.61 | convolution fusion | flops 2147745792 | bytes 11010048 | tf_op jit(solution)/shard_map/ri,rj->ij/dot_general | solution.py:71
  495.2 7.7 %fusion.165 = f32[4096,256]{1,0:T(8,128)} fusion(bf16[4096,1024]{1,0:T(8,128)(2,1)} %all-gather.2.cloned.1.call-done, bf16[1024,256]{1,0:T(8,128)(2,1)S(1)} %copy-done), kind=kOutput, calls=%fused_computation.217 | convolution fusion | flops 2147483648 | bytes 13107200 | tf_op jit(solution)/shard_map/dot_general | solution.py:73
  502.9 54.3 %reduce-scatter.4.cloned.1.call-done = bf16[128,256]{1,0:T(8,128)(2,1)} async-done(((bf16[1024,256]{1,0:T(8,128)(2,1)}), bf16[128,256]{1,0:T(8,128)(2,1)}) %reduce-scatter.4.cloned.1.call-update) | async-done | bytes 65552
  (118 shorter events, 117.3 us)
Async XLA Ops:
  7.2 488.0 %copy-start = (bf16[1024,256]{1,0:T(8,128)(2,1)S(1)}, bf16[1024,256]{1,0:T(8,128)(2,1)}, u32[]{:S(2)}) copy-start(bf16[1024,256]{1,0:T(8,128)(2,1)} %param.5) | copy-start | bytes 1572868
  7.2 8.1 %copy-start.1 = (bf16[32,128,256]{2,1,0:T(8,128)(2,1)S(1)}, bf16[32,128,256]{2,1,0:T(8,128)(2,1)}, u32[]{:S(2)}) copy-start(bf16[32,128,256]{2,1,0:T(8,128)(2,1)} %param.4) | copy-start | bytes 6291460
  7.2 481.2 %all-gather.2.cloned.1.call-start = ((), (), s32[]{:S(2)}) async-start(), calls=%async_computation.1 | async-start | bytes 10485760 | tf_op jit(solution)/shard_map/all_gather | solution.py:70
  9.1 47.9 %collective-permute-start = (bf16[1,4,4,128,256]{4,3,2,1,0:T(8,128)(2,1)S(1)}, bf16[1,4,4,128,256]{4,3,2,1,0:T(8,128)(2,1)S(1)}, u32[]{:S(2)}, u32[]{:S(2)}) collective-permute-start(bf16[1,4,4,128,256]{4,3,2,1,0:T(8,128)(2,1)S(1)} %bitcast.347), channel_id=1, source_target_pairs={{0,4},{4,8},{8,12},{12,16},{16,20},{20,24},{24,28},{28,0},{1,5},{5... | collective-permute-start | bytes 3145736 | tf_op jit(solution)/shard_map/ppermute | solution.py:23
  12.2 47.1 %collective-permute-start.1 = (bf16[1,4,4,128,256]{4,3,2,1,0:T(8,128)(2,1)S(1)}, bf16[1,4,4,128,256]{4,3,2,1,0:T(8,128)(2,1)S(1)}, u32[]{:S(2)}, u32[]{:S(2)}) collective-permute-start(bf16[1,4,4,128,256]{4,3,2,1,0:T(8,128)(2,1)S(1)} %bitcast.346), channel_id=1, source_target_pairs={{4,0},{8,4},{12,8},{16,12},{20,16},{24,20},{28,24},{0,28},{5,1},{9... | collective-permute-start | bytes 3145736 | tf_op jit(solution)/shard_map/ppermute | solution.py:25
  15.3 2.2 slice-start
  15.4 3.1 slice-start.1
  78.2 44.3 %collective-permute-start.2 = (bf16[1,4,4,128,256]{4,3,2,1,0:T(8,128)(2,1)S(1)}, bf16[1,4,4,128,256]{4,3,2,1,0:T(8,128)(2,1)S(1)}, u32[]{:S(2)}, u32[]{:S(2)}) collective-permute-start(bf16[1,4,4,128,256]{4,3,2,1,0:T(8,128)(2,1)S(1)} %bitcast.353), channel_id=1, source_target_pairs={{0,4},{4,8},{8,12},{12,16},{16,20},{20,24},{24,28},{28,0},{1,5},{5... | collective-permute-start | bytes 3145736 | tf_op jit(solution)/shard_map/ppermute | solution.py:23
  78.5 48.1 %collective-permute-start.3 = (bf16[1,4,4,128,256]{4,3,2,1,0:T(8,128)(2,1)S(1)}, bf16[1,4,4,128,256]{4,3,2,1,0:T(8,128)(2,1)S(1)}, u32[]{:S(2)}, u32[]{:S(2)}) collective-permute-start(bf16[1,4,4,128,256]{4,3,2,1,0:T(8,128)(2,1)S(1)} %bitcast.348), channel_id=1, source_target_pairs={{4,0},{8,4},{12,8},{16,12},{20,16},{24,20},{28,24},{0,28},{5,1},{9... | collective-permute-start | bytes 3145736 | tf_op jit(solution)/shard_map/ppermute | solution.py:25
  145.1 1.9 copy-start.2
  150.8 44.9 %collective-permute-start.4 = (bf16[1,4,4,128,256]{4,3,2,1,0:T(8,128)(2,1)S(1)}, bf16[1,4,4,128,256]{4,3,2,1,0:T(8,128)(2,1)S(1)}, u32[]{:S(2)}, u32[]{:S(2)}) collective-permute-start(bf16[1,4,4,128,256]{4,3,2,1,0:T(8,128)(2,1)S(1)} %bitcast.354), channel_id=1, source_target_pairs={{0,4},{4,8},{8,12},{12,16},{16,20},{20,24},{24,28},{28,0},{1,5},{5... | collective-permute-start | bytes 3145736 | tf_op jit(solution)/shard_map/ppermute | solution.py:23
  150.8 48.5 %collective-permute-start.5 = (bf16[1,4,4,128,256]{4,3,2,1,0:T(8,128)(2,1)S(1)}, bf16[1,4,4,128,256]{4,3,2,1,0:T(8,128)(2,1)S(1)}, u32[]{:S(2)}, u32[]{:S(2)}) collective-permute-start(bf16[1,4,4,128,256]{4,3,2,1,0:T(8,128)(2,1)S(1)} %bitcast.349), channel_id=1, source_target_pairs={{4,0},{8,4},{12,8},{16,12},{20,16},{24,20},{28,24},{0,28},{5,1},{9... | collective-permute-start | bytes 3145736 | tf_op jit(solution)/shard_map/ppermute | solution.py:25
  222.2 44.5 %collective-permute-start.6 = (bf16[1,4,4,128,256]{4,3,2,1,0:T(8,128)(2,1)S(1)}, bf16[1,4,4,128,256]{4,3,2,1,0:T(8,128)(2,1)S(1)}, u32[]{:S(2)}, u32[]{:S(2)}) collective-permute-start(bf16[1,4,4,128,256]{4,3,2,1,0:T(8,128)(2,1)S(1)} %bitcast.355), channel_id=1, source_target_pairs={{0,4},{4,8},{8,12},{12,16},{16,20},{20,24},{24,28},{28,0},{1,5},{5... | collective-permute-start | bytes 3145736 | tf_op jit(solution)/shard_map/ppermute | solution.py:23
  222.2 48.7 %collective-permute-start.7 = (bf16[1,4,4,128,256]{4,3,2,1,0:T(8,128)(2,1)S(1)}, bf16[1,4,4,128,256]{4,3,2,1,0:T(8,128)(2,1)S(1)}, u32[]{:S(2)}, u32[]{:S(2)}) collective-permute-start(bf16[1,4,4,128,256]{4,3,2,1,0:T(8,128)(2,1)S(1)} %bitcast.350), channel_id=1, source_target_pairs={{4,0},{8,4},{12,8},{16,12},{20,16},{24,20},{28,24},{0,28},{5,1},{9... | collective-permute-start | bytes 3145736 | tf_op jit(solution)/shard_map/ppermute | solution.py:25
  293.9 44.6 %collective-permute-start.8 = (bf16[1,4,4,128,256]{4,3,2,1,0:T(8,128)(2,1)S(1)}, bf16[1,4,4,128,256]{4,3,2,1,0:T(8,128)(2,1)S(1)}, u32[]{:S(2)}, u32[]{:S(2)}) collective-permute-start(bf16[1,4,4,128,256]{4,3,2,1,0:T(8,128)(2,1)S(1)} %bitcast.356), channel_id=1, source_target_pairs={{0,4},{4,8},{8,12},{12,16},{16,20},{20,24},{24,28},{28,0},{1,5},{5... | collective-permute-start | bytes 3145736 | tf_op jit(solution)/shard_map/ppermute | solution.py:23
  293.9 47.2 %collective-permute-start.9 = (bf16[1,4,4,128,256]{4,3,2,1,0:T(8,128)(2,1)S(1)}, bf16[1,4,4,128,256]{4,3,2,1,0:T(8,128)(2,1)S(1)}, u32[]{:S(2)}, u32[]{:S(2)}) collective-permute-start(bf16[1,4,4,128,256]{4,3,2,1,0:T(8,128)(2,1)S(1)} %bitcast.351), channel_id=1, source_target_pairs={{4,0},{8,4},{12,8},{16,12},{20,16},{24,20},{28,24},{0,28},{5,1},{9... | collective-permute-start | bytes 3145736 | tf_op jit(solution)/shard_map/ppermute | solution.py:25
  364.0 43.9 %collective-permute-start.10 = (bf16[1,4,4,128,256]{4,3,2,1,0:T(8,128)(2,1)S(1)}, bf16[1,4,4,128,256]{4,3,2,1,0:T(8,128)(2,1)S(1)}, u32[]{:S(2)}, u32[]{:S(2)}) collective-permute-start(bf16[1,4,4,128,256]{4,3,2,1,0:T(8,128)(2,1)S(1)} %bitcast.357), channel_id=1, source_target_pairs={{0,4},{4,8},{8,12},{12,16},{16,20},{20,24},{24,28},{28,0},{1,5},{5... | collective-permute-start | bytes 3145736 | tf_op jit(solution)/shard_map/ppermute | solution.py:23
  364.0 48.2 %collective-permute-start.11 = (bf16[1,4,4,128,256]{4,3,2,1,0:T(8,128)(2,1)S(1)}, bf16[1,4,4,128,256]{4,3,2,1,0:T(8,128)(2,1)S(1)}, u32[]{:S(2)}, u32[]{:S(2)}) collective-permute-start(bf16[1,4,4,128,256]{4,3,2,1,0:T(8,128)(2,1)S(1)} %bitcast.352), channel_id=1, source_target_pairs={{4,0},{8,4},{12,8},{16,12},{20,16},{24,20},{28,24},{0,28},{5,1},{9... | collective-permute-start | bytes 3145736 | tf_op jit(solution)/shard_map/ppermute | solution.py:25
  414.0 2.8 copy-start.4
  429.8 58.6 %copy-start.3 = (bf16[32,128,256]{2,1,0:T(8,128)(2,1)S(1)}, bf16[32,128,256]{2,1,0:T(8,128)(2,1)}, u32[]{:S(2)}) copy-start(bf16[32,128,256]{2,1,0:T(8,128)(2,1)} %fusion.3) | copy-start | bytes 6291460
  429.8 127.4 %reduce-scatter.4.cloned.1.call-start = ((), (), s32[]{:S(2)}) async-start(), calls=%async_computation.2 | async-start | bytes 589824
Sparse Core Ops, SparseCore 0:
  429.9 58.4 all-gather.1
  495.3 61.9 reduce-scatter.3
where the time goes:
time: 572 us; the launch traced here: 566 us
  waiting for transfers between devices  299 us (52%)
  matrix products  191 us (33%)
  starting transfers between devices  31 us (5%)
  other arithmetic  15.6 us (3%)
  between operations  14.7 us (3%)
  local copies, waits for them, and re-layouts  14.6 us (3%)
    dot_general x42, matrix products, apply_ham(): jnp.einsum('eij,ejo->eio', hamiltonian[:, direction], moved, preferred_el...  177 us
    ppermute x6, waiting for transfers between devices, extended(): lax.ppermute(tail, axis, [(i, (i + 1) % count) for i in range(count)])  166 us
    all_gather x1, waiting for transfers between devices, on_device(): panel_cols = lax.all_gather(filtered, 'orb', axis=1, tiled=True)  58.6 us
    unnamed x3, waiting for transfers between devices  54.3 us
    ppermute x6, starting transfers between devices, extended(): lax.ppermute(head, axis, [((i + 1) % count, i) for i in range(count)])  27.6 us
    ppermute x6, waiting for transfers between devices, extended(): lax.ppermute(head, axis, [((i + 1) % count, i) for i in range(count)])  20.9 us
  transfers between devices with their start and end apart: 14, of which 14 were waited for; matrix products, arithmetic and copies ran while one was open for 14% of the time, Pallas kernels for 0%

commit v1 on v0

--- a/solution.py
+++ b/solution.py
@@ -1,6 +1,10 @@
+import functools
+
 import jax
 import jax.numpy as jnp
 from jax import lax
+from jax.experimental import pallas as pl
+from jax.experimental.pallas import tpu as pltpu
 from jax.sharding import PartitionSpec as P
 
 NB = 128
@@ -53,11 +57,274 @@
     return accumulated
 
 
-def on_device(hamiltonian, start, ritz):
-    elem_count = hamiltonian.shape[0]
-    orb_cols = start.shape[2]
-    local_rows = elem_count * NB
-    rows_total = float(local_rows * lax.axis_size("elem"))
+PIECES = 4
+
+
+def filter_kernel(
+    n, layers, ham, start, out, blocks, vec, val, halo,
+    local, start_s, start_r, ham_s, ham_r, halo_s, halo_r, back_s, back_r,
+):
+    plane = GY * GZ
+    elem_local = layers * plane
+    half = start.shape[2] // 2
+    merged_layers = 2 * layers
+    group = plane // PIECES
+    me, orb = lax.axis_index("elem"), lax.axis_index("orb")
+    s = lax.rem(me, 2)
+    partner = me + 1 - 2 * s
+    left, right = lax.rem(me + n - 2, n), lax.rem(me + 2, n)
+    across = lax.rem(orb + 2, 4)
+    mate = orb + 1 - 2 * lax.rem(orb, 2)
+    diagonal = lax.rem(mate + 2, 4)
+
+    barrier = pltpu.get_barrier_semaphore()
+    for target in ({"elem": partner}, {"elem": left}, {"elem": right}, {"orb": across}, {"orb": mate}):
+        pl.semaphore_signal(barrier, inc=1, device_id=target, device_id_type=pl.DeviceIdType.MESH)
+
+    def lanes(part):
+        return pl.ds(pl.multiple_of(part * half, half), half)
+
+    def layer_of(side, first):
+        return side * first + (1 - side) * (1 - first)
+
+    own_h = pltpu.make_async_copy(ham, blocks.at[pl.ds(s * elem_local, elem_local)], local.at[0])
+    own_v = pltpu.make_async_copy(
+        start.at[:, :, lanes(s)], vec.at[0, pl.ds(s * elem_local, elem_local)], local.at[1]
+    )
+    own_v.start()
+    own_h.start()
+    pl.semaphore_wait(barrier, 5)
+
+    def start_copy(first):
+        base = layer_of(s, first) * plane
+        return pltpu.make_async_remote_copy(
+            src_ref=start.at[pl.ds(base, plane), :, lanes(1 - s)],
+            dst_ref=vec.at[0, pl.ds(s * elem_local + base, plane)],
+            send_sem=start_s.at[first], recv_sem=start_r.at[first],
+            device_id={"elem": partner}, device_id_type=pl.DeviceIdType.MESH,
+        )
+
+    def place(side, c, q):
+        first = 1 - c // PIECES
+        return side * elem_local + layer_of(side, first) * plane + lax.rem(c, PIECES) * group + q
+
+    def ham_y(c):
+        at = place(s, c, orb)
+        return pltpu.make_async_remote_copy(
+            src_ref=ham.at[at - s * elem_local], dst_ref=blocks.at[at],
+            send_sem=ham_s.at[0, c], recv_sem=ham_r.at[0, c],
+            device_id={"elem": partner}, device_id_type=pl.DeviceIdType.MESH,
+        )
+
+    def ham_on(kind, c, q, to):
+        at = place(1 - s, c, q)
+        return pltpu.make_async_remote_copy(
+            src_ref=blocks.at[at], dst_ref=blocks.at[at],
+            send_sem=ham_s.at[kind, c], recv_sem=ham_r.at[kind, c],
+            device_id={"orb": to}, device_id_type=pl.DeviceIdType.MESH,
+        )
+
+    def halo_copy(k, side, c):
+        layer = 0 if side == 1 else merged_layers - 1
+        return pltpu.make_async_remote_copy(
+            src_ref=vec.at[lax.rem(k, 2), pl.ds(layer * plane + c * group, group)],
+            dst_ref=halo.at[k, side, pl.ds(c * group, group)],
+            send_sem=halo_s.at[k, side, c], recv_sem=halo_r.at[k, side, c],
+            device_id={"elem": left if side == 1 else right}, device_id_type=pl.DeviceIdType.MESH,
+        )
+
+    start_copy(1).start()
+    start_copy(0).start()
+
+    @pl.loop(0, 2 * PIECES)
+    def _(c):
+        ham_y(c).start()
+
+    own_v.wait()
+    start_copy(1).wait_recv()
+
+    @pl.loop(0, PIECES)
+    def _(c):
+        halo_copy(0, 0, c).start()
+        halo_copy(0, 1, c).start()
+
+    start_copy(0).wait_recv()
+
+    @pl.loop(0, 2 * elem_local)
+    def _(i):
+        val[0, i] = vec[0, i].astype(jnp.float32)
+        val[1, i] = jnp.zeros((NB, half), jnp.float32)
+
+    own_h.wait()
+
+    def forward(c):
+        ham_y(c).wait_recv()
+        ham_on(1, c, orb, across).start()
+        ham_on(2, c, orb, mate).start()
+
+    def finish(c):
+        ham_on(1, c, across, across).wait_recv()
+        ham_on(3, c, across, mate).start()
+        ham_on(2, c, mate, mate).wait_recv()
+        ham_on(3, c, diagonal, mate).wait_recv()
+
+    def bring(first, last):
+        forward(first)
+
+        @pl.loop(first, last - 1)
+        def _(c):
+            forward(c + 1)
+            finish(c)
+
+        finish(last - 1)
+
+    def element(k, at, below, above):
+        now, later = lax.rem(k, 2), lax.rem(k + 1, 2)
+        j = lax.rem(at, plane)
+        base = at - j
+        jy, jz = j // GZ, lax.rem(j, GZ)
+        around = [
+            lax.rem(jy + GY - 1, GY) * GZ + jz,
+            lax.rem(jy + 1, GY) * GZ + jz,
+            jy * GZ + lax.rem(jz + GZ - 1, GZ),
+            jy * GZ + lax.rem(jz + 1, GZ),
+        ]
+        rhs = jnp.concatenate(
+            [vec[now, at], below, above] + [vec[now, base + other] for other in around], axis=0
+        )
+        lhs = jnp.concatenate([blocks[at, d] for d in range(7)], axis=1)
+        image = jnp.dot(lhs, rhs, preferred_element_type=jnp.float32)
+        first = k == 0
+        scale = jnp.where(first, 1.0 / half_width, 2.0 / half_width)
+        keep = jnp.where(first, 0.0, 1.0)
+        value = scale * (image - center_shift * val[now, at]) - keep * val[later, at]
+        val[later, at] = value
+        vec[later, at] = value.astype(jnp.bfloat16)
+
+    def edges(k, send):
+        now = lax.rem(k, 2)
+
+        @pl.loop(0, PIECES)
+        def _(c):
+            for side, layer in ((0, 0), (1, merged_layers - 1)):
+                halo_copy(k, side, c).wait_recv()
+
+                @pl.when(k >= 1)
+                def _():
+                    halo_copy(k - 1, 1 - side, c).wait_send()
+
+                for i in range(group):
+                    j = c * group + i
+                    at = layer * plane + j
+                    if side == 0:
+                        element(k, at, halo[k, 0, j], vec[now, at + plane])
+                    else:
+                        element(k, at, vec[now, at - plane], halo[k, 1, j])
+                if send:
+                    halo_copy(k + 1, 1 - side, c).start()
+
+    def interior(k):
+        now = lax.rem(k, 2)
+
+        @pl.loop(plane // group, (merged_layers - 1) * plane // group)
+        def _(c):
+            for i in range(group):
+                at = c * group + i
+                element(k, at, vec[now, at - plane], vec[now, at + plane])
+
+    bring(0, PIECES)
+
+    @pl.loop(0, DEG - 1)
+    def _(k):
+        edges(k, True)
+
+        @pl.when(k == 0)
+        def _():
+            bring(PIECES, 2 * PIECES)
+
+        interior(k)
+
+    last = DEG % 2
+
+    def back_copy(first):
+        base = layer_of(1 - s, first) * plane
+        return pltpu.make_async_remote_copy(
+            src_ref=vec.at[last, pl.ds((1 - s) * elem_local + base, plane)],
+            dst_ref=out.at[pl.ds(base, plane), :, lanes(s)],
+            send_sem=back_s.at[first], recv_sem=back_r.at[first],
+            device_id={"elem": partner}, device_id_type=pl.DeviceIdType.MESH,
+        )
+
+    def back_wait(first):
+        base = layer_of(s, first) * plane
+        return pltpu.make_async_remote_copy(
+            src_ref=vec.at[last, pl.ds(s * elem_local + base, plane)],
+            dst_ref=out.at[pl.ds(base, plane), :, lanes(1 - s)],
+            send_sem=back_s.at[first], recv_sem=back_r.at[first],
+            device_id={"elem": partner}, device_id_type=pl.DeviceIdType.MESH,
+        )
+
+    interior(DEG - 1)
+    back_copy(0).start()
+    edges(DEG - 1, False)
+    back_copy(1).start()
+    keep_own = pltpu.make_async_copy(
+        vec.at[last, pl.ds(s * elem_local, elem_local)], out.at[:, :, lanes(s)], local.at[1]
+    )
+    keep_own.start()
+
+    @pl.loop(0, 2 * PIECES)
+    def _(c):
+        ham_y(c).wait_send()
+        ham_on(1, c, orb, across).wait_send()
+        ham_on(2, c, orb, mate).wait_send()
+        ham_on(3, c, across, mate).wait_send()
+
+    @pl.loop(0, PIECES)
+    def _(c):
+        halo_copy(DEG - 1, 0, c).wait_send()
+        halo_copy(DEG - 1, 1, c).wait_send()
+
+    for first in (0, 1):
+        start_copy(first).wait_send()
+        back_copy(first).wait_send()
+        back_wait(first).wait_recv()
+    keep_own.wait()
+
+
+def merged_filter(hamiltonian, start):
+    n = lax.axis_size("elem")
+    elem_local, _, orb_cols = start.shape
+    layers = elem_local // (GY * GZ)
+    half = orb_cols // 2
+    dma = pltpu.SemaphoreType.DMA
+    return pl.pallas_call(
+        functools.partial(filter_kernel, n, layers),
+        out_shape=jax.ShapeDtypeStruct(start.shape, jnp.bfloat16),
+        in_specs=[pl.BlockSpec(memory_space=pl.ANY)] * 2,
+        out_specs=pl.BlockSpec(memory_space=pl.ANY),
+        scratch_shapes=[
+            pltpu.VMEM((2 * elem_local, 7, NB, NB), jnp.bfloat16),
+            pltpu.VMEM((2, 2 * elem_local, NB, half), jnp.bfloat16),
+            pltpu.VMEM((2, 2 * elem_local, NB, half), jnp.float32),
+            pltpu.VMEM((DEG, 2, GY * GZ, NB, half), jnp.bfloat16),
+            dma((2,)),
+            dma((2,)), dma((2,)),
+            dma((4, 2 * PIECES)), dma((4, 2 * PIECES)),
+            dma((DEG, 2, PIECES)), dma((DEG, 2, PIECES)),
+            dma((2,)), dma((2,)),
+        ],
+        compiler_params=pltpu.CompilerParams(
+            collective_id=0, has_side_effects=True, vmem_limit_bytes=48 * 1024 * 1024
+        ),
+        cost_estimate=pl.CostEstimate(
+            flops=2 * DEG * 7 * elem_local * NB * NB * orb_cols,
+            bytes_accessed=hamiltonian.size * 2 + start.size * 4, transcendentals=0,
+        ),
+    )(hamiltonian, start)
+
+
+def plain_filter(hamiltonian, start):
     previous = start.astype(jnp.float32)
     current = (apply_ham(hamiltonian, start) - center_shift * previous) / half_width
     for degree in range(DEG - 1):
@@ -66,7 +333,21 @@
         following = 2.0 / half_width * (image - center_shift * current) - previous
         previous = current
         current = following
-    filtered = current.astype(jnp.bfloat16).reshape(local_rows, orb_cols)
+    return current.astype(jnp.bfloat16)
+
+
+def on_device(hamiltonian, start, ritz):
+    elem_count = hamiltonian.shape[0]
+    orb_cols = start.shape[2]
+    local_rows = elem_count * NB
+    rows_total = float(local_rows * lax.axis_size("elem"))
+    slabs = lax.axis_size("elem")
+    can_merge = (
+        slabs % 2 == 0 and slabs >= 6 and lax.axis_size("orb") == 4
+        and orb_cols % 256 == 0 and elem_count == 2 * GY * GZ
+    )
+    filtered = (merged_filter if can_merge else plain_filter)(hamiltonian, start)
+    filtered = filtered.reshape(local_rows, orb_cols)
     panel_cols = lax.all_gather(filtered, "orb", axis=1, tiled=True)
     block_part = jnp.einsum("ri,rj->ij", filtered, panel_cols, preferred_element_type=jnp.float32)
     margin_rows = block_part

time: 572 us -> 349 us (0.61); the launches traced: 566 us -> 349 us
  Pallas kernels: 0 us -> 205 us
  waiting for transfers between devices: 299 us -> 111 us
  matrix products: 191 us -> 14.1 us
  starting transfers between devices: 31 us -> 0.08 us
  other arithmetic: 15.6 us -> 0.67 us
  local copies, waits for them, and re-layouts: 14.6 us -> 3.63 us
    pallas_call x0 -> x1, Pallas kernels: none -> 205 us  [merged_filter(): pl.pallas_call(functools.partial(filter_kernel, n, layers), out_shape=jax...]
    ppermute x12 -> x0, waiting for transfers between devices: 186 us -> none  [the longest x6 166 us: extended(): lax.ppermute(tail, axis, [(i, (i + 1) % count) for i in range(count)])]
    dot_general x42 -> x0, matrix products: 177 us -> none  [apply_ham(): jnp.einsum('eij,ejo->eio', hamiltonian[:, direction], moved, preferred_el...]
    ppermute x12 -> x0, starting transfers between devices: 30.9 us -> none  [the longest x6 27.6 us: extended(): lax.ppermute(head, axis, [((i + 1) % count, i) for i in range(count)])]
    concatenate x28 -> x0, other arithmetic: 14.9 us -> none  [the longest x6 10.5 us: extended(): jnp.concatenate([lax.ppermute(tail, axis, [(i, (i + 1) % count) for i in...]
    slice x30 -> x0, local copies, waits for them, and re-layouts: 9.8 us -> none  [the longest x12 4.12 us: apply_ham(): jnp.roll(element_grid, 1, axis=2)]
  transfers between devices with their start and end apart: 14 -> 2, of which waited for: 14 -> 2; matrix products, arithmetic and copies ran while one was open for 14% -> 2% of each run, Pallas kernels for 0% -> 0%
where the time goes in v1:
time: 349 us
  Pallas kernels  205 us (59%)
  waiting for transfers between devices  111 us (32%)
  matrix products  14.1 us (4%)
  between operations  14.1 us (4%)
  local copies, waits for them, and re-layouts  3.63 us (1%)
    pallas_call x1, Pallas kernels, merged_filter(): pl.pallas_call(functools.partial(filter_kernel, n, layers), out_shape=jax...  205 us
    all_gather x1, waiting for transfers between devices, on_device(): panel_cols = lax.all_gather(filtered, 'orb', axis=1, tiled=True)  57.1 us
    unnamed x3, waiting for transfers between devices  54.3 us
    dot_general x1, matrix products, on_device(): rotated_part = jnp.dot(panel_cols, ritz, preferred_element_type=jnp.float32)  7.74 us
  transfers between devices with their start and end apart: 2, of which 2 were waited for; matrix products, arithmetic and copies ran while one was open for 2% of the time, Pallas kernels for 0%

profile of v1, /device:TPU:0, one launch (start us, length us, event | category | flops | bytes accessed | tf_op | source)
XLA Modules:
  0.0 348.9 jit_solution(14903946977006598515)
XLA Ops:
  7.2 0.0 copy-start
  7.2 0.0 all-gather.2.cloned.1.call-start
  7.2 0.0 copy-start.1
  7.2 1.6 copy-done.1
  8.9 204.9 %shard_map.50 = bf16[32,128,256]{2,1,0:T(8,128)(2,1)} custom-call(bf16[32,7,128,128]{3,2,1,0:T(8,128)(2,1)} %ham.1, bf16[32,128,256]{2,1,0:T(8,128)(2,1)S(1)} %copy-done.1), custom_call_target="tpu_custom_call" | custom-call | flops 11274289152 | bytes 11534336 | tf_op jit(solution)/shard_map/pallas_call | solution.py:301
  213.8 0.0 all-gather.2.cloned.1.call-update
  213.8 0.0 reduce-scatter.4.cloned.1.call-start
  213.8 57.1 %all-gather.2.cloned.1.call-done = bf16[4096,1024]{1,0:T(8,128)(2,1)} async-done(((bf16[4096,256]{1,0:T(8,128)(2,1)}), bf16[4096,1024]{1,0:T(8,128)(2,1)}) %all-gather.2.cloned.1.call-update) | async-done | bytes 8388624 | tf_op jit(solution)/shard_map/all_gather | solution.py:351
  270.9 6.4 %convolution_convert_fusion = bf16[256,1024]{1,0:T(8,128)(2,1)S(1)} fusion(bf16[4096,256]{1,0:T(8,128)(2,1)} %bitcast, bf16[4096,1024]{1,0:T(8,128)(2,1)} %all-gather.2.cloned.1.call-done), kind=kOutput, calls=%fused_computation | convolution fusion | flops 2147745792 | bytes 11010048 | tf_op jit(solution)/shard_map/ri,rj->ij/dot_general | solution.py:352
  277.3 1.0 copy.5
  278.3 0.0 reduce-scatter.4.cloned.1.call-update
  278.4 0.0 copy-done
  278.4 7.7 %fusion = f32[4096,256]{1,0:T(8,128)} fusion(bf16[4096,1024]{1,0:T(8,128)(2,1)} %all-gather.2.cloned.1.call-done, bf16[1024,256]{1,0:T(8,128)(2,1)S(1)} %copy-done), kind=kOutput, calls=%fused_computation.2 | convolution fusion | flops 2147483648 | bytes 13107200 | tf_op jit(solution)/shard_map/dot_general | solution.py:354
  286.1 54.3 %reduce-scatter.4.cloned.1.call-done = bf16[128,256]{1,0:T(8,128)(2,1)} async-done(((bf16[1024,256]{1,0:T(8,128)(2,1)}), bf16[128,256]{1,0:T(8,128)(2,1)}) %reduce-scatter.4.cloned.1.call-update) | async-done | bytes 65552
  340.4 0.9 copy.6
  341.4 0.7 convert_multiply_fusion
Async XLA Ops:
  7.2 271.2 %copy-start = (bf16[1024,256]{1,0:T(8,128)(2,1)S(1)}, bf16[1024,256]{1,0:T(8,128)(2,1)}, u32[]{:S(2)}) copy-start(bf16[1024,256]{1,0:T(8,128)(2,1)} %param.5) | copy-start | bytes 1572868
  7.2 263.7 %all-gather.2.cloned.1.call-start = ((), (), s32[]{:S(2)}) async-start(), calls=%async_computation.1 | async-start | bytes 10485760 | tf_op jit(solution)/shard_map/all_gather | solution.py:351
  7.2 1.6 copy-start.1
  213.8 126.6 %reduce-scatter.4.cloned.1.call-start = ((), (), s32[]{:S(2)}) async-start(), calls=%async_computation.2 | async-start | bytes 589824
Sparse Core Ops, SparseCore 0:
  213.9 56.9 all-gather.1
  278.5 61.9 reduce-scatter.3

commit v2 on v1

--- a/solution.py
+++ b/solution.py
@@ -61,8 +61,8 @@
 
 
 def filter_kernel(
-    n, layers, ham, start, out, blocks, vec, val, halo,
-    local, start_s, start_r, ham_s, ham_r, halo_s, halo_r, back_s, back_r,
+    n, layers, ham, start, ritz, margin, rotated, blocks, vec, val, halo, panel, turn, product, total, parts, came,
+    local, start_s, start_r, ham_s, ham_r, halo_s, halo_r, gather_s, gather_r, part_s, part_r, out_s,
 ):
     plane = GY * GZ
     elem_local = layers * plane
@@ -78,7 +78,8 @@
     diagonal = lax.rem(mate + 2, 4)
 
     barrier = pltpu.get_barrier_semaphore()
-    for target in ({"elem": partner}, {"elem": left}, {"elem": right}, {"orb": across}, {"orb": mate}):
+    peers = [{"elem": lax.rem(me + d, n)} for d in range(1, n)]
+    for target in peers + [{"orb": across}, {"orb": mate}]:
         pl.semaphore_signal(barrier, inc=1, device_id=target, device_id_type=pl.DeviceIdType.MESH)
 
     def lanes(part):
@@ -93,7 +94,9 @@
     )
     own_v.start()
     own_h.start()
-    pl.semaphore_wait(barrier, 5)
+    own_r = pltpu.make_async_copy(ritz, turn, local.at[2])
+    own_r.start()
+    pl.semaphore_wait(barrier, n + 1)
 
     def start_copy(first):
         base = layer_of(s, first) * plane
@@ -201,7 +204,7 @@
         val[later, at] = value
         vec[later, at] = value.astype(jnp.bfloat16)
 
-    def edges(k, send):
+    def edges(k, after):
         now = lax.rem(k, 2)
 
         @pl.loop(0, PIECES)
@@ -220,8 +223,10 @@
                         element(k, at, halo[k, 0, j], vec[now, at + plane])
                     else:
                         element(k, at, vec[now, at - plane], halo[k, 1, j])
-                if send:
+                if after is None:
                     halo_copy(k + 1, 1 - side, c).start()
+            if after is not None:
+                after(c)
 
     def interior(k):
         now = lax.rem(k, 2)
@@ -236,7 +241,7 @@
 
     @pl.loop(0, DEG - 1)
     def _(k):
-        edges(k, True)
+        edges(k, None)
 
         @pl.when(k == 0)
         def _():
@@ -246,32 +251,110 @@
 
     last = DEG % 2
 
-    def back_copy(first):
-        base = layer_of(1 - s, first) * plane
-        return pltpu.make_async_remote_copy(
-            src_ref=vec.at[last, pl.ds((1 - s) * elem_local + base, plane)],
-            dst_ref=out.at[pl.ds(base, plane), :, lanes(s)],
-            send_sem=back_s.at[first], recv_sem=back_r.at[first],
+    def rows(side, c):
+        return layer_of(side, c // PIECES) * plane + lax.rem(c, PIECES) * group
+
+    def to_partner(c):
+        at = rows(1 - s, c)
+        return pltpu.make_async_remote_copy(
+            src_ref=vec.at[last, pl.ds((1 - s) * elem_local + at, group)],
+            dst_ref=panel.at[2 * orb + s, pl.ds(at, group)],
+            send_sem=gather_s.at[0, c], recv_sem=gather_r.at[0, c],
             device_id={"elem": partner}, device_id_type=pl.DeviceIdType.MESH,
         )
 
-    def back_wait(first):
-        base = layer_of(s, first) * plane
-        return pltpu.make_async_remote_copy(
-            src_ref=vec.at[last, pl.ds(s * elem_local + base, plane)],
-            dst_ref=out.at[pl.ds(base, plane), :, lanes(1 - s)],
-            send_sem=back_s.at[first], recv_sem=back_r.at[first],
-            device_id={"elem": partner}, device_id_type=pl.DeviceIdType.MESH,
+    def to_orb(kind, h, c):
+        block = 2 * (across if kind == 2 else orb) + (s if h == 0 else 1 - s)
+        at = panel.at[block, pl.ds(rows(s, c), group)]
+        return pltpu.make_async_remote_copy(
+            src_ref=at, dst_ref=at,
+            send_sem=gather_s.at[1 + 2 * kind + h, c], recv_sem=gather_r.at[1 + 2 * kind + h, c],
+            device_id={"orb": across if kind == 0 else mate}, device_id_type=pl.DeviceIdType.MESH,
+        )
+
+    def offer(c):
+        to_partner(c).start()
+        at = rows(s, c)
+        panel[2 * orb + s, pl.ds(at, group)] = vec[last, pl.ds(s * elem_local + at, group)]
+        to_orb(0, 0, c).start()
+        to_orb(1, 0, c).start()
+
+    def pass_on(c):
+        to_partner(c).wait_recv()
+        to_orb(0, 1, c).start()
+        to_orb(1, 1, c).start()
+
+    def relay(c):
+        for h in (0, 1):
+            to_orb(0, h, c).wait_recv()
+            to_orb(2, h, c).start()
+
+    def complete(c):
+        for kind in (1, 2):
+            for h in (0, 1):
+                to_orb(kind, h, c).wait_recv()
+
+    def result_copy(c):
+        at = pl.ds(rows(s, c), group)
+        return pltpu.make_async_copy(product.at[at], rotated.at[at], out_s.at[c])
+
+    def multiply(c):
+        at = pl.ds(rows(s, c), group)
+        whole = jnp.concatenate([panel[b, at].reshape(group * NB, half) for b in range(n)], axis=1)
+        mine = jnp.concatenate(
+            [panel[2 * orb + h, at].reshape(group * NB, half) for h in (0, 1)], axis=1
+        )
+        result = jnp.dot(whole, turn[...], preferred_element_type=jnp.float32)
+        product[at] = result.reshape(group, NB, 2 * half)
+        result_copy(c).start()
+        total[...] += lax.dot_general(
+            mine, whole, (((0,), (0,)), ((), ())), preferred_element_type=jnp.float32
         )
 
     interior(DEG - 1)
-    back_copy(0).start()
-    edges(DEG - 1, False)
-    back_copy(1).start()
-    keep_own = pltpu.make_async_copy(
-        vec.at[last, pl.ds(s * elem_local, elem_local)], out.at[:, :, lanes(s)], local.at[1]
-    )
-    keep_own.start()
+
+    @pl.loop(0, PIECES)
+    def _(c):
+        offer(c)
+
+    total[...] = jnp.zeros_like(total)
+
+    def after(c):
+        offer(PIECES + c)
+        pass_on(c)
+
+    edges(DEG - 1, after)
+    own_r.wait()
+    relay(0)
+
+    @pl.loop(0, PIECES)
+    def _(c):
+        pass_on(PIECES + c)
+        relay(c + 1)
+        complete(c)
+        multiply(c)
+
+    @pl.loop(PIECES, 2 * PIECES)
+    def _(c):
+        @pl.when(c + 1 < 2 * PIECES)
+        def _():
+            relay(c + 1)
+
+        complete(c)
+        multiply(c)
+
+    def part_copy(d):
+        to = lax.rem(me + d, n)
+        return pltpu.make_async_remote_copy(
+            src_ref=parts.at[to], dst_ref=came.at[d - 1],
+            send_sem=part_s.at[d - 1], recv_sem=part_r.at[d - 1],
+            device_id={"elem": to}, device_id_type=pl.DeviceIdType.MESH,
+        )
+
+    for i in range(n):
+        parts[i] = total[:, i * half : (i + 1) * half].astype(jnp.bfloat16)
+    for d in range(1, n):
+        part_copy(d).start()
 
     @pl.loop(0, 2 * PIECES)
     def _(c):
@@ -279,6 +362,11 @@
         ham_on(1, c, orb, across).wait_send()
         ham_on(2, c, orb, mate).wait_send()
         ham_on(3, c, across, mate).wait_send()
+        to_partner(c).wait_send()
+        for kind in range(3):
+            for h in (0, 1):
+                to_orb(kind, h, c).wait_send()
+        result_copy(c).wait()
 
     @pl.loop(0, PIECES)
     def _(c):
@@ -287,12 +375,16 @@
 
     for first in (0, 1):
         start_copy(first).wait_send()
-        back_copy(first).wait_send()
-        back_wait(first).wait_recv()
-    keep_own.wait()
-
-
-def merged_filter(hamiltonian, start):
+    sums = total[:, lanes(me)]
+    for d in range(1, n):
+        part_copy(d).wait_recv()
+        sums = sums + came[d - 1].astype(jnp.float32)
+    margin[...] = sums / float(n * elem_local * NB)
+    for d in range(1, n):
+        part_copy(d).wait_send()
+
+
+def merged(hamiltonian, start, ritz):
     n = lax.axis_size("elem")
     elem_local, _, orb_cols = start.shape
     layers = elem_local // (GY * GZ)
@@ -300,28 +392,39 @@
     dma = pltpu.SemaphoreType.DMA
     return pl.pallas_call(
         functools.partial(filter_kernel, n, layers),
-        out_shape=jax.ShapeDtypeStruct(start.shape, jnp.bfloat16),
-        in_specs=[pl.BlockSpec(memory_space=pl.ANY)] * 2,
-        out_specs=pl.BlockSpec(memory_space=pl.ANY),
+        out_shape=(
+            jax.ShapeDtypeStruct((orb_cols, half), jnp.float32),
+            jax.ShapeDtypeStruct(start.shape, jnp.float32),
+        ),
+        in_specs=[pl.BlockSpec(memory_space=pl.ANY)] * 3,
+        out_specs=(pl.BlockSpec(memory_space=pltpu.VMEM), pl.BlockSpec(memory_space=pl.ANY)),
         scratch_shapes=[
             pltpu.VMEM((2 * elem_local, 7, NB, NB), jnp.bfloat16),
             pltpu.VMEM((2, 2 * elem_local, NB, half), jnp.bfloat16),
             pltpu.VMEM((2, 2 * elem_local, NB, half), jnp.float32),
             pltpu.VMEM((DEG, 2, GY * GZ, NB, half), jnp.bfloat16),
-            dma((2,)),
+            pltpu.VMEM((n, elem_local, NB, half), jnp.bfloat16),
+            pltpu.VMEM(ritz.shape, jnp.bfloat16),
+            pltpu.VMEM(start.shape, jnp.float32),
+            pltpu.VMEM((orb_cols, n * half), jnp.float32),
+            pltpu.VMEM((n, orb_cols, half), jnp.bfloat16),
+            pltpu.VMEM((n - 1, orb_cols, half), jnp.bfloat16),
+            dma((3,)),
             dma((2,)), dma((2,)),
             dma((4, 2 * PIECES)), dma((4, 2 * PIECES)),
             dma((DEG, 2, PIECES)), dma((DEG, 2, PIECES)),
-            dma((2,)), dma((2,)),
+            dma((7, 2 * PIECES)), dma((7, 2 * PIECES)),
+            dma((n - 1,)), dma((n - 1,)),
+            dma((2 * PIECES,)),
         ],
         compiler_params=pltpu.CompilerParams(
-            collective_id=0, has_side_effects=True, vmem_limit_bytes=48 * 1024 * 1024
+            collective_id=0, has_side_effects=True, vmem_limit_bytes=60 * 1024 * 1024
         ),
         cost_estimate=pl.CostEstimate(
-            flops=2 * DEG * 7 * elem_local * NB * NB * orb_cols,
-            bytes_accessed=hamiltonian.size * 2 + start.size * 4, transcendentals=0,
+            flops=2 * elem_local * NB * orb_cols * (DEG * 7 * NB + 2 * n * half),
+            bytes_accessed=hamiltonian.size * 2 + start.size * 6, transcendentals=0,
         ),
-    )(hamiltonian, start)
+    )(hamiltonian, start, ritz)
 
 
 def plain_filter(hamiltonian, start):
@@ -344,9 +447,11 @@
     slabs = lax.axis_size("elem")
     can_merge = (
         slabs % 2 == 0 and slabs >= 6 and lax.axis_size("orb") == 4
-        and orb_cols % 256 == 0 and elem_count == 2 * GY * GZ
+        and orb_cols == 2 * NB and ritz.shape[0] == slabs * NB and elem_count == 2 * GY * GZ
     )
-    filtered = (merged_filter if can_merge else plain_filter)(hamiltonian, start)
+    if can_merge:
+        return merged(hamiltonian, start, ritz)
+    filtered = plain_filter(hamiltonian, start)
     filtered = filtered.reshape(local_rows, orb_cols)
     panel_cols = lax.all_gather(filtered, "orb", axis=1, tiled=True)
     block_part = jnp.einsum("ri,rj->ij", filtered, panel_cols, preferred_element_type=jnp.float32)

time: 349 us -> 249 us (0.71)
  waiting for transfers between devices: 111 us -> 0 us
  Pallas kernels: 205 us -> 241 us
  matrix products: 14.1 us -> 0 us
  between operations: 14.1 us -> 0.64 us
    all_gather x1 -> x0, waiting for transfers between devices: 57.1 us -> none  [on_device(): panel_cols = lax.all_gather(filtered, 'orb', axis=1, tiled=True)]
    unnamed x3 -> x0, waiting for transfers between devices: 54.3 us -> none
    pallas_call x1, Pallas kernels: 205 us -> 241 us  [merged(): pl.pallas_call(functools.partial(filter_kernel, n, layers), out_shape=(ja...]
    dot_general x2 -> x0, matrix products: 14.1 us -> none  [the longest x1 7.74 us: on_device(): rotated_part = jnp.dot(panel_cols, ritz, preferred_element_type=jnp.float32)]
  transfers between devices with their start and end apart: 2 -> 0, of which waited for: 2 -> 0; matrix products, arithmetic and copies ran while one was open for 2% -> 0% of each run, Pallas kernels for 0% -> 0%
where the time goes in v2:
time: 249 us; the launch traced here: 248 us
  Pallas kernels  241 us (97%)
  local copies, waits for them, and re-layouts  6.22 us (2%)
    pallas_call x1, Pallas kernels, merged(): pl.pallas_call(functools.partial(filter_kernel, n, layers), out_shape=(ja...  241 us
    unnamed x2, local copies, waits for them, and re-layouts  6.22 us

profile of v2, /device:TPU:0, one launch (start us, length us, event | category | flops | bytes accessed | tf_op | source)
XLA Modules:
  0.0 247.8 jit_solution(3873150845877931642)
XLA Ops:
  0.6 241.0 %shard_map.50 = (f32[256,128]{1,0:T(8,128)}, f32[32,128,256]{2,1,0:T(8,128)}) custom-call(bf16[32,7,128,128]{3,2,1,0:T(8,128)(2,1)} %ham.1, bf16[32,128,256]{2,1,0:T(8,128)(2,1)} %start.1, bf16[1024,256]{1,0:T(8,128)(2,1)} %ritz.1), custom_call_target="tpu_custom_call" | custom-call | flops 15569256448 | bytes 13631488 | tf_op jit(solution)/shard_map/pallas_call | solution.py:393
  241.6 1.6 copy.7
  243.2 4.7 %copy.8 = f32[32,128,256]{2,1,0:T(8,128)} copy(f32[32,128,256]{2,1,0:T(8,128)} %get-tuple-element.5) | data formatting | bytes 8388608
